TPU v7x, 32 devices: a whole 2x2x4 slice. The times are simulated.
32 devices in a mesh: section: 8 (over z, x), expert: 4 (over y, core).
Axes of the slice: x: 2, y: 2, z: 4, core: 2. Of those that a mesh axis runs over, the one named last changes fastest.
Arguments:
- tokens: bfloat16 [1024, 4096], P('expert', 'section'), may hold values from -6 to 6
- routes: int32 [1024, 2], P('expert'), may hold values from 0 to 3, all different within a row; in each aligned block of 256 rows (0 to 255, 256 to 511, ...) at most 160 rows name the same one
- mix_weights: float32 [1024, 2], P('expert'), may hold values from 0.2 to 1
- w_gate: bfloat16 [4, 4096, 8192], P('expert', None, 'section'), may hold values from -0.125 to 0.125
- w_up: bfloat16 [4, 4096, 8192], P('expert', None, 'section'), may hold values from -0.125 to 0.125
- w_down: bfloat16 [4, 8192, 4096], P('expert', 'section'), may hold values from -0.09375 to 0.09375
- upstream: bfloat16 [1024, 4096], P('expert', 'section'), may hold values from -6 to 6
Outputs:
- mixed: bfloat16 [1024, 4096], P('expert', 'section')
- grad_tokens: bfloat16 [1024, 4096], P('expert', 'section')
- grad_mix: float32 [1024, 2], P('expert')
- grad_gate: bfloat16 [4, 4096, 8192], P('expert', None, 'section')
- grad_up: bfloat16 [4, 4096, 8192], P('expert', None, 'section')
- grad_down: bfloat16 [4, 8192, 4096], P('expert', 'section')
Inputs may be any that keep to these rules, and one draw needn't show every extreme that they name: `routes`: each token names 2 different experts. Among the 256 tokens of one index of the expert axis no expert is named more than 160 times, and in some such block one expert is named exactly 160 times.
All inputs are finite; a program needn't handle non-finite values.
Results may differ from a plain program's by a relative error of at most 0.02.
Values may be sent and summed in bfloat16 or wider, within the bound.
A program may use at most 128 MiB of HBM per device.

v0:
```python
import jax
import jax.numpy as jnp
from jax import lax
from jax.sharding import PartitionSpec as P

highest = lax.Precision.HIGHEST


def slot_tables(route_rows, mix_rows, capacity, experts):
    tok_count, top_count = route_rows.shape
    flat_routes = route_rows.reshape(-1)
    onehot = (flat_routes[:, None] == jnp.arange(experts, dtype=jnp.int32)[None, :]).astype(
        jnp.int32
    )
    earlier = jnp.cumsum(onehot, axis=0) - onehot
    position = jnp.sum(earlier * onehot, axis=1)
    target = (flat_routes * capacity + position).reshape(tok_count, top_count)
    slot_ids = jnp.arange(experts * capacity, dtype=jnp.int32)
    hits = target[None, :, :] == slot_ids[:, None, None]
    matches = hits.astype(jnp.float32)
    select = jnp.sum(matches, axis=2)
    weighted = jnp.sum(matches * mix_rows[None, :, :], axis=2)
    token_ids = jnp.arange(tok_count, dtype=jnp.int32)
    slot_token = jnp.sum(jnp.sum(hits.astype(jnp.int32), axis=2) * token_ids[None, :], axis=1)
    return (target, select, weighted, slot_token)


def per_device(tokens, routes, mix_weights, w_gate, w_up, w_down, upstream):
    experts = lax.axis_size("expert")
    tok_count = tokens.shape[0]
    top_count = routes.shape[1]
    capacity = 5 * tok_count * top_count // (4 * experts)
    slot_total = experts * capacity
    target, select, weighted, slot_token = slot_tables(routes, mix_weights, capacity, experts)
    slot_fill = jnp.sum(select, axis=1)
    slot_scale = jnp.sum(weighted, axis=1)
    gate_local = w_gate[0]
    up_local = w_up[0]
    down_local = w_down[0]

    def collect(source, factor):
        taken = source[slot_token].astype(jnp.float32)
        return (taken * factor[:, None]).astype(jnp.bfloat16)

    def to_experts(source, factor):
        block = collect(source, factor)
        arrived = lax.all_to_all(
            block.reshape(experts, capacity, -1), "expert", split_axis=0, concat_axis=0, tiled=True
        )
        whole = lax.all_gather(arrived, "section", axis=2, tiled=True)
        return whole.reshape(slot_total, -1)

    def to_sources(partial_value):
        summed = lax.psum_scatter(
            partial_value.reshape(experts, capacity, -1).astype(jnp.bfloat16),
            "section",
            scatter_dimension=2,
            tiled=True,
        )
        back = lax.all_to_all(summed, "expert", split_axis=0, concat_axis=0, tiled=True)
        return back.reshape(slot_total, -1)

    dispatched = to_experts(tokens, slot_fill)
    act_gate = jnp.dot(dispatched, gate_local, preferred_element_type=jnp.float32)
    act_up = jnp.dot(dispatched, up_local, preferred_element_type=jnp.float32)
    sig = jax.nn.sigmoid(act_gate)
    silu_gate = act_gate * sig
    hidden = (silu_gate * act_up).astype(jnp.bfloat16)
    partial_value = jnp.dot(hidden, down_local, preferred_element_type=jnp.float32)
    returned = to_sources(partial_value).astype(jnp.float32)
    moe_out = jnp.dot(weighted.T, returned, precision=highest)
    mixed = (tokens.astype(jnp.float32) + moe_out).astype(jnp.bfloat16)
    picked = returned[target]
    upstream_wide = upstream.astype(jnp.float32)
    mix_terms = jnp.einsum("tkd,td->tk", picked, upstream_wide, precision=highest)
    grad_mix = lax.psum(mix_terms, "section")
    grad_rows = to_experts(upstream, slot_scale)
    grad_hidden = lax.dot_general(
        grad_rows, down_local, (((1,), (1,)), ((), ())), preferred_element_type=jnp.float32
    )
    grad_down = lax.dot_general(
        hidden, grad_rows, (((0,), (0,)), ((), ())), preferred_element_type=jnp.float32
    ).astype(jnp.bfloat16)
    dsilu = sig * (1.0 + act_gate * (1.0 - sig))
    grad_act_gate = (grad_hidden * act_up * dsilu).astype(jnp.bfloat16)
    grad_act_up = (grad_hidden * silu_gate).astype(jnp.bfloat16)
    grad_gate = lax.dot_general(
        dispatched, grad_act_gate, (((0,), (0,)), ((), ())), preferred_element_type=jnp.float32
    ).astype(jnp.bfloat16)
    grad_up = lax.dot_general(
        dispatched, grad_act_up, (((0,), (0,)), ((), ())), preferred_element_type=jnp.float32
    ).astype(jnp.bfloat16)
    first = lax.dot_general(
        grad_act_gate, gate_local, (((1,), (1,)), ((), ())), preferred_element_type=jnp.float32
    )
    second = lax.dot_general(
        grad_act_up, up_local, (((1,), (1,)), ((), ())), preferred_element_type=jnp.float32
    )
    back_rows = to_sources(first + second).astype(jnp.float32)
    grad_moe = jnp.dot(select.T, back_rows, precision=highest)
    grad_tokens = (upstream_wide + grad_moe).astype(jnp.bfloat16)
    return (mixed, grad_tokens, grad_mix, grad_gate[None], grad_up[None], grad_down[None])


def solution(mesh):
    return jax.shard_map(
        per_device,
        mesh=mesh,
        in_specs=(
            P("expert", "section"),
            P("expert", None),
            P("expert", None),
            P("expert", None, "section"),
            P("expert", None, "section"),
            P("expert", "section", None),
            P("expert", "section"),
        ),
        out_specs=(
            P("expert", "section"),
            P("expert", "section"),
            P("expert", None),
            P("expert", None, "section"),
            P("expert", None, "section"),
            P("expert", "section", None),
        ),
        check_vma=False,
    )
```

profile of v0, /device:TPU:0, one launch (start us, length us, event | category | flops | bytes accessed | tf_op | source)
XLA Modules:
  0.0 482.6 jit_solution(11901000220814041175)
XLA Ops:
  7.2 0.0 copy-start.1
  7.2 0.0 all-gather.5.cloned.1.call-start
  7.2 0.8 copy.25
  8.1 0.1 eq.42
  8.2 0.1 eq.38
  8.4 1.2 reduce-window.6
  9.6 0.2 slice_reduce_fusion
  9.8 0.2 reduce-window.9
  10.0 0.1 add_bitcast_fusion
  10.1 0.1 reduce_sum.68
  10.3 0.1 copy.27
  10.3 0.7 compare_select_fusion.1
  11.0 0.3 convert_reduce_fusion.2
  11.3 1.2 select_reduce_fusion
  12.5 0.0 copy-start
  12.5 0.2 multiply_reduce_fusion
  12.7 0.1 mul.83
  12.8 0.0 copy-done.1
  12.8 2.8 gather_fusion.1
  15.6 0.2 fusion.18
  15.8 14.4 %all_to_all.20 = bf16[4,160,512]{2,1,0:T(8,128)(2,1)} all-to-all(bf16[4,160,512]{2,1,0:T(8,128)(2,1)S(1)} %fusion.18), channel_id=1, replica_groups=mesh['section'=8,'expert'=4] {'expert'}, dimensions={0} | all-to-all | bytes 1310720 | tf_op jit(solution)/shard_map/all_to_all | solution.py:47
  30.2 0.0 all-gather.5.cloned.1.call-update
  30.2 0.0 all-gather.3.cloned.1.call-start
  30.3 0.0 copy-done
  30.3 2.8 gather_fusion
  33.1 0.1 mul.78
  33.2 0.2 fusion.19
  33.4 13.3 %all_to_all.21 = bf16[4,160,512]{2,1,0:T(8,128)(2,1)} all-to-all(bf16[4,160,512]{2,1,0:T(8,128)(2,1)S(1)} %fusion.19), channel_id=1, replica_groups=mesh['section'=8,'expert'=4] {'expert'}, dimensions={0} | all-to-all | bytes 1310720 | tf_op jit(solution)/shard_map/all_to_all | solution.py:47
  46.7 0.0 all-gather.3.cloned.1.call-update
  46.7 0.2 reduce-scatter.3.cloned.1.call-start
  47.0 71.3 %all-gather.5.cloned.1.call-done = bf16[4,160,4096]{2,1,0:T(8,128)(2,1)} async-done(((bf16[4,160,512]{2,1,0:T(8,128)(2,1)}), bf16[4,160,4096]{2,1,0:T(8,128)(2,1)}) %all-gather.5.cloned.1.call-update) | async-done | bytes 5242896 | tf_op jit(solution)/shard_map/all_gather | solution.py:50
  118.3 10.6 %fusion.2 = f32[640,1024]{1,0:T(8,128)} fusion(bf16[640,4096]{1,0:T(8,128)(2,1)} %bitcast.87, bf16[1,1024,4096]{2,1,0:T(8,128)(2,1)} %param.12), kind=kOutput, calls=%fused_computation.6 | convolution fusion | flops 5368709120 | bytes 16252928 | tf_op jit(solution)/shard_map/dot_general | solution.py:78
  128.9 76.8 %all-gather.3.cloned.1.call-done = bf16[4,160,4096]{2,1,0:T(8,128)(2,1)} async-done(((bf16[4,160,512]{2,1,0:T(8,128)(2,1)}), bf16[4,160,4096]{2,1,0:T(8,128)(2,1)}) %all-gather.3.cloned.1.call-update) | async-done | bytes 5242896 | tf_op jit(solution)/shard_map/all_gather | solution.py:50
  205.8 9.7 %fusion.6 = f32[640,1024]{1,0:T(8,128)S(1)} fusion(bf16[640,4096]{1,0:T(8,128)(2,1)} %bitcast.89, bf16[1,4096,1024]{2,1,0:T(8,128)(2,1)} %param.11), kind=kOutput, calls=%fused_computation.10 | convolution fusion | flops 5368709120 | bytes 16252928 | tf_op jit(solution)/shard_map/dot_general | solution.py:65
  215.4 0.0 copy-done.2
  215.4 0.0 copy-done.6
  215.4 0.0 slice-start.1
  215.5 10.4 %multiply_convert_fusion.1 = (bf16[640,1024]{1,0:T(8,128)(2,1)}, bf16[640,1024]{1,0:T(8,128)(2,1)}, bf16[640,1024]{1,0:T(8,128)(2,1)S(1)}) fusion(f32[640,1024]{1,0:T(8,128)S(1)} %copy-done.6, f32[640,1024]{1,0:T(8,128)S(1)} %fusion.6, bf16[640,4096]{1,0:T(8,128)(2,1)S(1)} %bitcast.92, bf16[1,4096,1024]{2,1,0:T(8,128)(2,1)} %param.10), kind=kOutput, calls=%fused_computation.21 | convolution fusion | flops 5378539520 | bytes 22806528 | tf_op jit(solution)/shard_map/dot_general | solution.py:64
  225.9 1.1 copy-done.3
  226.9 7.3 %fusion.12 = bf16[4,160,4096]{2,1,0:T(8,128)(2,1)} fusion(bf16[4,160,1024]{2,1,0:T(8,128)(2,1)S(1)} %bitcast.93, bf16[1,1024,4096]{2,1,0:T(8,128)(2,1)S(1)} %bitcast.86), kind=kOutput, calls=%fused_computation.19 | convolution fusion | flops 5371330560 | bytes 14942208 | tf_op jit(solution)/shard_map/dot_general | solution.py:69
  234.2 0.0 reduce-scatter.3.cloned.1.call-update
  234.3 0.3 reduce-scatter.5.cloned.1.call-start
  234.5 0.0 copy-start.5
  234.6 11.9 %fusion.4 = f32[640,4096]{1,0:T(8,128)} fusion(bf16[640,1024]{1,0:T(8,128)(2,1)} %get-tuple-element.13, bf16[1,4096,1024]{2,1,0:T(8,128)(2,1)} %param.11), kind=kOutput, calls=%fused_computation.8 | convolution fusion | flops 5368709120 | bytes 20185088 | tf_op jit(solution)/shard_map/dot_general | solution.py:96
  246.4 12.4 %add_convert_fusion = bf16[640,4096]{1,0:T(8,128)(2,1)} fusion(f32[640,4096]{1,0:T(8,128)} %fusion.4, bf16[640,1024]{1,0:T(8,128)(2,1)S(1)} %copy-done.5, bf16[1,4096,1024]{2,1,0:T(8,128)(2,1)} %param.10), kind=kOutput, calls=%fused_computation.3 | convolution fusion | flops 5373952000 | bytes 25427968 | tf_op jit(solution)/shard_map/dot_general | solution.py:93
  258.8 0.0 reduce-scatter.5.cloned.1.call-update
  258.9 0.1 copy.28
  259.0 0.1 reshape.113
  259.2 12.0 %convert_bitcast_fusion.2 = bf16[1,4096,1024]{2,1,0:T(8,128)(2,1)} fusion(bf16[640,4096]{1,0:T(8,128)(2,1)} %bitcast.90, bf16[640,1024]{1,0:T(8,128)(2,1)} %get-tuple-element.12), kind=kOutput, calls=%fused_computation.18 | convolution fusion | flops 5372903424 | bytes 14942208 | tf_op jit(solution)/shard_map/dot_general | solution.py:87
  271.1 11.5 %convert_bitcast_fusion.1 = bf16[1,4096,1024]{2,1,0:T(8,128)(2,1)} fusion(bf16[640,4096]{1,0:T(8,128)(2,1)} %bitcast.91, bf16[640,1024]{1,0:T(8,128)(2,1)S(1)} %copy-done.4), kind=kOutput, calls=%fused_computation.17 | convolution fusion | flops 5372903424 | bytes 14942208 | tf_op jit(solution)/shard_map/dot_general | solution.py:90
  282.6 53.0 %reduce-scatter.3.cloned.1.call-done = bf16[4,160,512]{2,1,0:T(8,128)(2,1)} async-done(((bf16[4,160,4096]{2,1,0:T(8,128)(2,1)}), bf16[4,160,512]{2,1,0:T(8,128)(2,1)}) %reduce-scatter.3.cloned.1.call-update) | async-done | bytes 655376 | tf_op jit(solution)/shard_map/reduce_scatter | solution.py:54
  335.6 3.5 all-to-all-start.1
  339.1 11.7 %convert_bitcast_fusion = bf16[1,1024,4096]{2,1,0:T(8,128)(2,1)} fusion(bf16[640,1024]{1,0:T(8,128)(2,1)} %copy-done.3, bf16[640,4096]{1,0:T(8,128)(2,1)} %bitcast.88), kind=kOutput, calls=%fused_computation.16 | convolution fusion | flops 5372903424 | bytes 14942208 | tf_op jit(solution)/shard_map/dot_general | solution.py:81
  350.8 91.2 %reduce-scatter.5.cloned.1.call-done = bf16[4,160,512]{2,1,0:T(8,128)(2,1)} async-done(((bf16[4,160,4096]{2,1,0:T(8,128)(2,1)}), bf16[4,160,512]{2,1,0:T(8,128)(2,1)}) %reduce-scatter.5.cloned.1.call-update) | async-done | bytes 655376 | tf_op jit(solution)/shard_map/reduce_scatter | solution.py:54
  442.0 0.0 all-to-all-done.1
  442.0 3.5 all-to-all-start.3
  445.5 2.6 gather_fusion.2
  448.1 2.1 reshape.112
  450.1 2.0 fusion.22
  452.1 0.1 copy.30
  452.2 20.7 %psum.7 = f32[256,2]{0,1:T(2,128)} all-reduce(f32[256,2]{0,1:T(2,128)S(1)} %bitcast.83), channel_id=1, replica_groups=mesh['section'=8,'expert'=4] {'section'}, use_global_device_ids=true, to_apply=%region_11.12 | all-reduce | flops 512 | bytes 4096 | tf_op jit(solution)/shard_map/psum | solution.py:76
  473.0 1.5 fusion.20
  474.5 0.0 all-to-all-done.3
  474.5 1.5 fusion.21
  (15 shorter events, 0.1 us)
Async XLA Ops:
  7.2 5.6 %copy-start.1 = (bf16[256,512]{1,0:T(8,128)(2,1)S(1)}, bf16[256,512]{1,0:T(8,128)(2,1)}, u32[]{:S(2)}) copy-start(bf16[256,512]{1,0:T(8,128)(2,1)} %param.13) | copy-start | bytes 786436
  7.2 111.1 %all-gather.5.cloned.1.call-start = ((), (), s32[]{:S(2)}) async-start(), calls=%async_computation.8 | async-start | bytes 5898240 | tf_op jit(solution)/shard_map/all_gather | solution.py:50
  12.5 17.8 %copy-start = (bf16[256,512]{1,0:T(8,128)(2,1)S(1)}, bf16[256,512]{1,0:T(8,128)(2,1)}, u32[]{:S(2)}) copy-start(bf16[256,512]{1,0:T(8,128)(2,1)} %param.7) | copy-start | bytes 786436
  30.2 175.5 %all-gather.3.cloned.1.call-start = ((), (), s32[]{:S(2)}) async-start(), calls=%async_computation.6 | async-start | bytes 5898240 | tf_op jit(solution)/shard_map/all_gather | solution.py:50
  46.7 288.9 %reduce-scatter.3.cloned.1.call-start = ((), (), s32[]{:S(2)}) async-start(), calls=%async_computation.7 | async-start | bytes 5898240 | tf_op jit(solution)/shard_map/reduce_scatter | solution.py:54
  205.8 9.7 %copy-start.2 = (bf16[4,160,4096]{2,1,0:T(8,128)(2,1)S(1)}, bf16[4,160,4096]{2,1,0:T(8,128)(2,1)}, u32[]{:S(2)}) copy-start(bf16[4,160,4096]{2,1,0:T(8,128)(2,1)} %all-gather.3.cloned.1.call-done) | copy-start | bytes 15728644
  205.8 9.7 %copy-start.6 = (f32[640,1024]{1,0:T(8,128)S(1)}, f32[640,1024]{1,0:T(8,128)}, u32[]{:S(2)}) copy-start(f32[640,1024]{1,0:T(8,128)} %fusion.2) | copy-start | bytes 7864324
  205.8 21.1 %slice-start = ((s8[8388608]{0:T(1024)(128)(4,1)}), s8[4194304]{0:T(1024)(128)(4,1)S(1)}, s32[]{:S(2)}) async-start(s8[8388608]{0:T(1024)(128)(4,1)} %bitcast.85), calls=%async_computation.10 | async-start | bytes 8388608
  215.4 11.5 %slice-start.1 = ((s8[8388608]{0:T(1024)(128)(4,1)}), s8[4194304]{0:T(1024)(128)(4,1)S(1)}, s32[]{:S(2)}) async-start(s8[8388608]{0:T(1024)(128)(4,1)} %bitcast.85), calls=%async_computation.11 | async-start | bytes 8388608
  225.9 1.1 copy-start.3
  234.3 207.7 %reduce-scatter.5.cloned.1.call-start = ((), (), s32[]{:S(2)}) async-start(), calls=%async_computation.9 | async-start | bytes 5898240 | tf_op jit(solution)/shard_map/reduce_scatter | solution.py:54
  234.5 11.9 %copy-start.5 = (bf16[640,1024]{1,0:T(8,128)(2,1)S(1)}, bf16[640,1024]{1,0:T(8,128)(2,1)}, u32[]{:S(2)}) copy-start(bf16[640,1024]{1,0:T(8,128)(2,1)} %get-tuple-element.12) | copy-start | bytes 3932164
  259.2 12.0 %copy-start.4 = (bf16[640,1024]{1,0:T(8,128)(2,1)S(1)}, bf16[640,1024]{1,0:T(8,128)(2,1)}, u32[]{:S(2)}) copy-start(bf16[640,1024]{1,0:T(8,128)(2,1)} %get-tuple-element.13) | copy-start | bytes 3932164
  335.6 106.4 %all-to-all-start.1 = ((bf16[4,160,512]{2,1,0:T(8,128)(2,1)}), bf16[4,160,512]{2,1,0:T(8,128)(2,1)S(1)}, u32[]{:S(2)}, u32[]{:S(2)}) async-start(bf16[4,160,512]{2,1,0:T(8,128)(2,1)} %reduce-scatter.3.cloned.1.call-done), calls=%async_computation.2 | async-start | bytes 1310720 | tf_op jit(solution)/shard_map/all_to_all | solution.py:60
  442.0 32.5 %all-to-all-start.3 = ((bf16[4,160,512]{2,1,0:T(8,128)(2,1)}), bf16[4,160,512]{2,1,0:T(8,128)(2,1)S(1)}, u32[]{:S(2)}, u32[]{:S(2)}) async-start(bf16[4,160,512]{2,1,0:T(8,128)(2,1)} %reduce-scatter.5.cloned.1.call-done), calls=%async_computation.5 | async-start | bytes 1310720 | tf_op jit(solution)/shard_map/all_to_all | solution.py:60
Sparse Core Ops, SparseCore 0:
  30.3 87.8 all-gather.4
  120.3 85.3 all-gather.2
  234.4 101.1 reduce-scatter.2
  339.1 102.8 reduce-scatter.4
where the time goes:
time: 483 us
  waiting for transfers between devices  292 us (60%)
  matrix products  103 us (21%)
  blocking collectives  48.5 us (10%)
  between operations  14 us (3%)
  local copies, waits for them, and re-layouts  13.4 us (3%)
  starting transfers between devices  7.53 us (2%)
    all_gather x2, waiting for transfers between devices, to_experts(): whole = lax.all_gather(arrived, 'section', axis=2, tiled=True)  148 us
    reduce_scatter x2, waiting for transfers between devices, to_sources(): lax.psum_scatter(partial_value.reshape(experts, capacity, -1).astype(jnp....  144 us
    all_to_all x2, blocking collectives, to_experts(): lax.all_to_all(block.reshape(experts, capacity, -1), 'expert', split_axis...  27.7 us
    psum x1, blocking collectives, per_device(): grad_mix = lax.psum(mix_terms, 'section')  20.7 us
    dot_general x1, matrix products, per_device(): lax.dot_general(grad_act_gate, gate_local, (((1,), (1,)), ((), ())), pref...  12.4 us
    dot_general x1, matrix products, per_device(): lax.dot_general(dispatched, grad_act_gate, (((0,), (0,)), ((), ())), pref...  12 us
    dot_general x1, matrix products, per_device(): lax.dot_general(grad_act_up, up_local, (((1,), (1,)), ((), ())), preferre...  11.9 us
    dot_general x1, matrix products, per_device(): lax.dot_general(hidden, grad_rows, (((0,), (0,)), ((), ())), preferred_el...  11.7 us
  transfers between devices with their start and end apart: 6, of which 4 were waited for; matrix products, arithmetic and copies ran while one was open for 17% of the time, Pallas kernels for 0%

commit v1 on v0

--- a/solution.py
+++ b/solution.py
@@ -1,9 +1,518 @@
+import functools
 import jax
 import jax.numpy as jnp
 from jax import lax
+from jax.experimental import pallas as pl
+from jax.experimental.pallas import tpu as pltpu
 from jax.sharding import PartitionSpec as P
 
 highest = lax.Precision.HIGHEST
+MESH = pl.DeviceIdType.MESH
+VMEM_BYTES = 60 * 1024 * 1024
+
+
+class Place:
+    def __init__(self, sections):
+        section, expert = lax.axis_index("section"), lax.axis_index("expert")
+        self.sections, self.lines = sections, sections // 2
+        self.z, self.x = lax.div(section, 2), lax.rem(section, 2)
+        self.y, self.core = lax.div(expert, 2), lax.rem(expert, 2)
+        self.expert = expert
+
+    def device(self, x=None, y=None, z=None, core=None):
+        x = self.x if x is None else x
+        y = self.y if y is None else y
+        z = self.z if z is None else z
+        core = self.core if core is None else core
+        return (2 * z + x, 2 * y + core)
+
+    def block(self, x, y, z, core):
+        return (2 * y + core) * self.sections + 2 * z + x
+
+    def greet(self, others):
+        barrier = pltpu.get_barrier_semaphore()
+        for other in others:
+            pl.semaphore_signal(barrier, inc=1, device_id=other, device_id_type=MESH)
+        for step in (1, -1):
+
+            @pl.when((self.z + step >= 0) & (self.z + step < self.lines))
+            def _():
+                pl.semaphore_signal(
+                    barrier, inc=1, device_id=self.device(z=self.z + step), device_id_type=MESH
+                )
+
+        ends = jnp.where(self.z > 0, 1, 0) + jnp.where(self.z < self.lines - 1, 1, 0)
+        pl.semaphore_wait(barrier, len(others) + ends)
+
+
+def gather_kernel(
+    sections, experts, cap, meta_ref, tok_ref, up_ref, x_ref, u_ref, sel_ref, mix_ref,
+    tok_all, up_all, meta_all, send_sem, recv_sem, meta_send, meta_recv,
+):
+    here = Place(sections)
+    x, y, z, core, lines = here.x, here.y, here.z, here.core, here.lines
+    held = (tok_all, up_all)
+    rows, width = tok_ref.shape
+    others = [(2 * z + x, lax.rem(here.expert + j, experts)) for j in range(1, experts)]
+    here.greet(others + [here.device(x=1 - x)])
+
+    def copy(a, block, link, target):
+        return pltpu.make_async_remote_copy(
+            src_ref=held[a].at[block],
+            dst_ref=held[a].at[block],
+            send_sem=send_sem.at[a, block, link],
+            recv_sem=recv_sem.at[a, block],
+            device_id=target,
+            device_id_type=MESH,
+        )
+
+    def meta_copy(j):
+        return pltpu.make_async_remote_copy(
+            src_ref=meta_all.at[here.expert],
+            dst_ref=meta_all.at[here.expert],
+            send_sem=meta_send.at[j],
+            recv_sem=meta_recv.at[here.expert],
+            device_id=others[j],
+            device_id_type=MESH,
+        )
+
+    own = here.block(x, y, z, core)
+    tok_all[own] = tok_ref[...]
+    up_all[own] = up_ref[...]
+    meta_all[here.expert] = meta_ref[...]
+    for j in range(experts - 1):
+        meta_copy(j).start()
+    buddy = here.device(core=1 - core)
+    near = (
+        (here.device(x=1 - x), here.device(y=1 - y)),
+        (here.device(y=1 - y), here.device(x=1 - x)),
+    )
+
+    def sends(d, sign, begin, wait):
+        zz = z + sign * d
+
+        def along(a, block, step):
+            @pl.when((z + step >= 0) & (z + step < lines))
+            def _():
+                begin(copy(a, block, 0 if step > 0 else 1, here.device(z=z + step)))
+
+        for a in range(2):
+            block = here.block(x, y, zz, core)
+            if d > 0:
+                wait(a, block)
+                along(a, block, -sign)
+            else:
+                along(a, block, 1)
+                along(a, block, -1)
+            begin(copy(a, block, 2, near[a][0]))
+            begin(copy(a, block, 3, near[a][1]))
+            begin(copy(a, block, 4, buddy))
+        for a in range(2):
+            block = here.block(1 - x, y, zz, core) if a == 0 else here.block(x, 1 - y, zz, core)
+            wait(a, block)
+            begin(copy(a, block, 3, near[a][1]))
+            begin(copy(a, block, 4, buddy))
+
+    def last(d, sign, begin, wait):
+        zz = z + sign * d
+        for a in range(2):
+            first = here.block(x, 1 - y, zz, core) if a == 0 else here.block(1 - x, y, zz, core)
+            for block in (first, here.block(1 - x, 1 - y, zz, core)):
+                wait(a, block)
+                begin(copy(a, block, 4, buddy))
+
+    def walk(begin, wait):
+        steps = [(d, sign) for d in range(lines) for sign in ((1,) if d == 0 else (1, -1))]
+        queue = [(sends, *steps[0])]
+        for before, after in zip(steps, steps[1:]):
+            queue += [(sends, *after), (last, *before)]
+        queue.append((last, *steps[-1]))
+        for part, d, sign in queue:
+            zz = z + sign * d
+            pl.when((zz >= 0) & (zz < lines))(functools.partial(part, d, sign, begin, wait))
+
+    def arrive(a, block):
+        copy(a, block, 4, buddy).wait_recv()
+
+    walk(lambda c: c.start(), arrive)
+
+    for j in range(experts - 1):
+        source = lax.rem(here.expert + j + 1, experts)
+        pltpu.make_async_remote_copy(
+            src_ref=meta_all.at[source],
+            dst_ref=meta_all.at[source],
+            send_sem=meta_send.at[j],
+            recv_sem=meta_recv.at[source],
+            device_id=others[j],
+            device_id_type=MESH,
+        ).wait_recv()
+    ids = (lax.broadcasted_iota(jnp.int32, (cap, rows), 0) + here.expert * cap).astype(jnp.float32)
+    for b in range(experts):
+        table = meta_all[b]
+        first = jnp.where(ids == table[0:1, :], 1.0, 0.0)
+        second = jnp.where(ids == table[1:2, :], 1.0, 0.0)
+        sel_ref[b * cap : (b + 1) * cap, :] = (first + second).astype(jnp.bfloat16)
+        mix_ref[b * cap : (b + 1) * cap, :] = jnp.sum(
+            first * table[2:3, :] + second * table[3:4, :], axis=1, keepdims=True
+        )
+
+    @pl.loop(0, sections)
+    def _(s):
+        for a in range(2):
+            for half in range(experts // 2):
+                arrive(a, (2 * half + 1 - core) * sections + s)
+
+    @pl.loop(0, sections)
+    def _(s):
+        columns = pl.ds(pl.multiple_of(s * width, width), width)
+        for b in range(experts):
+            take = sel_ref[b * cap : (b + 1) * cap, :]
+            for source, out in ((tok_all, x_ref), (up_all, u_ref)):
+                out[b * cap : (b + 1) * cap, columns] = jnp.dot(
+                    take, source[b * sections + s], preferred_element_type=jnp.float32
+                ).astype(jnp.bfloat16)
+
+    walk(lambda c: c.wait_send(), lambda a, block: None)
+    for j in range(experts - 1):
+        meta_copy(j).wait_send()
+
+
+def gather_rows(meta, tokens, upstream, sections, experts, cap):
+    rows, width = tokens.shape
+    total = experts * cap
+    blocks = sections * experts
+    vmem = pl.BlockSpec(memory_space=pltpu.VMEM)
+    return pl.pallas_call(
+        functools.partial(gather_kernel, sections, experts, cap),
+        out_shape=(
+            jax.ShapeDtypeStruct((total, width * sections), jnp.bfloat16),
+            jax.ShapeDtypeStruct((total, width * sections), jnp.bfloat16),
+            jax.ShapeDtypeStruct((total, rows), jnp.bfloat16),
+            jax.ShapeDtypeStruct((total, 1), jnp.float32),
+        ),
+        in_specs=[vmem] * 3,
+        out_specs=[vmem] * 4,
+        scratch_shapes=[
+            pltpu.VMEM((blocks, rows, width), jnp.bfloat16),
+            pltpu.VMEM((blocks, rows, width), jnp.bfloat16),
+            pltpu.VMEM((experts,) + meta.shape, jnp.float32),
+            pltpu.SemaphoreType.DMA((2, blocks, 5)),
+            pltpu.SemaphoreType.DMA((2, blocks)),
+            pltpu.SemaphoreType.DMA((experts,)),
+            pltpu.SemaphoreType.DMA((experts,)),
+        ],
+        compiler_params=pltpu.CompilerParams(
+            collective_id=0, has_side_effects=True, vmem_limit_bytes=VMEM_BYTES
+        ),
+        name="gather_rows",
+    )(meta, tokens, upstream)
+
+
+def return_kernel(
+    sections, experts, cap, y_ref, z_ref, sel_ref, dot_ref, tok_ref, up_ref,
+    mixed_ref, gtok_ref, gmix_ref,
+    out, mate, acc, got1, got2, got_up, got_down, tab_out, tab_in,
+    mate_s, mate_r, one_s, one_r, two_s, two_r, up_s, up_r, down_s, down_r, tab_s, tab_r,
+):
+    here = Place(sections)
+    x, y, z, core, lines = here.x, here.y, here.z, here.core, here.lines
+    rows, width = tok_ref.shape
+    parts = (y_ref, z_ref)
+    buddy = here.device(core=1 - core)
+    partners = [buddy, here.device(x=1 - x), here.device(y=1 - y)]
+    far, reach = [], 1
+    while reach < lines:
+        swapped = z + reach - 2 * reach * lax.rem(lax.div(z, reach), 2)
+        partners.append(here.device(z=swapped))
+        if reach > 1:
+            far.append(here.device(z=swapped))
+        reach *= 2
+    here.greet(partners[:3] + far)
+
+    def remote(src, dst, send, recv, target):
+        return pltpu.make_async_remote_copy(
+            src_ref=src, dst_ref=dst, send_sem=send, recv_sem=recv, device_id=target,
+            device_id_type=MESH,
+        )
+
+    def flip(value, turned):
+        return 1 - value if turned else value
+
+    def number(fx, fy, zz):
+        return flip(y, fy) * sections + 2 * zz + flip(x, fx)
+
+    def to_tokens(a, fx, fy, zz, which):
+        b = 2 * flip(y, fy) + which
+        at = pl.ds(pl.multiple_of(b * cap, 16), cap)
+        columns = pl.ds(pl.multiple_of((2 * zz + flip(x, fx)) * width, width), width)
+        return lax.dot_general(
+            sel_ref[at, :], parts[a][at, columns], (((0,), (0,)), ((), ())),
+            preferred_element_type=jnp.float32,
+        )
+
+    def to_mate(a, fx, fy, zz):
+        q = number(fx, fy, zz)
+        return remote(out.at[a, q], mate.at[a, q], mate_s.at[a, q], mate_r.at[a, q], buddy)
+
+    def to_first(a, fx, fy, zz):
+        q = number(fx, fy, zz)
+        slot = (flip(x, fx) if a == 0 else flip(y, fy)) * lines + zz
+        target = here.device(y=1 - y) if a == 0 else here.device(x=1 - x)
+        return remote(acc.at[a, q], got1.at[a, slot], one_s.at[a, slot], one_r.at[a, slot], target)
+
+    def to_second(a, fx, fy, zz):
+        q = number(fx, fy, zz)
+        target = here.device(x=1 - x) if a == 0 else here.device(y=1 - y)
+        return remote(acc.at[a, q], got2.at[a, zz], two_s.at[a, zz], two_r.at[a, zz], target)
+
+    def to_up(a, zz):
+        return remote(
+            acc.at[a, number(0, 0, zz)], got_up.at[a, zz], up_s.at[a, zz], up_r.at[a, zz],
+            here.device(z=z + 1),
+        )
+
+    def to_down(a, zz):
+        return remote(
+            acc.at[a, number(0, 0, zz)], got_down.at[a, zz], down_s.at[a, zz], down_r.at[a, zz],
+            here.device(z=z - 1),
+        )
+
+    def add(a, q, *terms):
+        value = acc[a, q].astype(jnp.float32)
+        for term in terms:
+            value = value + term.astype(jnp.float32)
+        acc[a, q] = value.astype(jnp.bfloat16)
+
+    def table_copy(i):
+        return remote(tab_out.at[i], tab_in.at[i], tab_s.at[i], tab_r.at[i], partners[i])
+
+    def table_step(i):
+        table_copy(i).wait_recv()
+        tab_out[i + 1] = tab_out[i] + tab_in[i]
+        if i + 1 < len(partners):
+            table_copy(i + 1).start()
+
+    line = lax.broadcasted_iota(jnp.int32, (8, rows), 0)
+    for b in range(experts):
+        at = slice(b * cap, (b + 1) * cap)
+        sums = jnp.sum(sel_ref[at, :].astype(jnp.float32) * dot_ref[at, :], axis=0, keepdims=True)
+        tab_out[0, b] = jnp.where(line == here.expert, sums, 0.0)
+    table_copy(0).start()
+
+    def offer(fx, fy):
+        @pl.loop(0, lines)
+        def _(zz):
+            for a in range(2):
+                out[a, number(fx, fy, zz)] = to_tokens(a, fx, fy, zz, 1 - core).astype(jnp.bfloat16)
+                to_mate(a, fx, fy, zz).start()
+
+    def join(fx, fy):
+        @pl.loop(0, lines)
+        def _(zz):
+            for a in range(2):
+                q = number(fx, fy, zz)
+                mine = to_tokens(a, fx, fy, zz, core)
+                to_mate(a, fx, fy, zz).wait_recv()
+                acc[a, q] = (mine + mate[a, q].astype(jnp.float32)).astype(jnp.bfloat16)
+                if fy if a == 0 else fx:
+                    to_first(a, fx, fy, zz).start()
+
+    offer(1, 1)
+    offer(0, 1)
+    join(1, 1)
+    offer(1, 0)
+    join(0, 1)
+    offer(0, 0)
+    join(1, 0)
+    join(0, 0)
+    table_step(0)
+
+    @pl.loop(0, lines)
+    def _(zz):
+        for a in range(2):
+            fx, fy = (1, 0) if a == 0 else (0, 1)
+            to_first(a, fx, fy, zz).wait_recv()
+            slot = (1 - x if a == 0 else 1 - y) * lines + zz
+            add(a, number(fx, fy, zz), got1[a, slot])
+            to_second(a, fx, fy, zz).start()
+
+    table_step(1)
+
+    @pl.loop(0, lines)
+    def _(zz):
+        for a in range(2):
+            to_first(a, 0, 0, zz).wait_recv()
+            slot = (x if a == 0 else y) * lines + zz
+            add(a, number(0, 0, zz), got1[a, slot])
+
+    table_step(2)
+
+    def both(do):
+        for up, down in zip(range(lines - 1, 0, -1), range(lines - 1)):
+
+            @pl.when(z < up)
+            def _():
+                for a in range(2):
+                    do(a, up, True)
+
+            @pl.when(z > down)
+            def _():
+                for a in range(2):
+                    do(a, down, False)
+
+    def pass_on(a, zz, rising):
+        to_second(a, 0, 0, zz).wait_recv()
+        q = number(0, 0, zz)
+        add(a, q, got2[a, zz])
+        if rising:
+
+            @pl.when(z > 0)
+            def _():
+                to_up(a, zz).wait_recv()
+                add(a, q, got_up[a, zz])
+
+            to_up(a, zz).start()
+        else:
+
+            @pl.when(z < lines - 1)
+            def _():
+                to_down(a, zz).wait_recv()
+                add(a, q, got_down[a, zz])
+
+            to_down(a, zz).start()
+
+    both(pass_on)
+    for i in range(3, len(partners)):
+        table_step(i)
+    gmix_ref[...] = tab_out[len(partners), here.expert]
+
+    for a, (base, result) in enumerate(((tok_ref, mixed_ref), (up_ref, gtok_ref))):
+        to_second(a, 0, 0, z).wait_recv()
+        q = number(0, 0, z)
+        add(a, q, got2[a, z])
+
+        @pl.when(z > 0)
+        def _():
+            to_up(a, z).wait_recv()
+            add(a, q, got_up[a, z])
+
+        @pl.when(z < lines - 1)
+        def _():
+            to_down(a, z).wait_recv()
+            add(a, q, got_down[a, z])
+
+        result[...] = (base[...].astype(jnp.float32) + acc[a, q].astype(jnp.float32)).astype(
+            jnp.bfloat16
+        )
+
+    @pl.loop(0, lines)
+    def _(zz):
+        for a in range(2):
+            for fx in (0, 1):
+                for fy in (0, 1):
+                    to_mate(a, fx, fy, zz).wait_send()
+                    if fy if a == 0 else fx:
+                        to_first(a, fx, fy, zz).wait_send()
+            to_second(a, 1 - a, a, zz).wait_send()
+
+    both(lambda a, zz, rising: (to_up(a, zz) if rising else to_down(a, zz)).wait_send())
+    for i in range(len(partners)):
+        table_copy(i).wait_send()
+
+
+def return_rows(part_y, part_z, select, inner, tokens, upstream, sections, experts, cap):
+    rows, width = tokens.shape
+    lines, half = sections // 2, sections * experts // 2
+    steps = 3 + (lines - 1).bit_length()
+    vmem = pl.BlockSpec(memory_space=pltpu.VMEM)
+    dma = pltpu.SemaphoreType.DMA
+
+    def blocks(count):
+        return pltpu.VMEM((2, count, rows, width), jnp.bfloat16)
+
+    return pl.pallas_call(
+        functools.partial(return_kernel, sections, experts, cap),
+        out_shape=(
+            jax.ShapeDtypeStruct(tokens.shape, jnp.bfloat16),
+            jax.ShapeDtypeStruct(tokens.shape, jnp.bfloat16),
+            jax.ShapeDtypeStruct((8, rows), jnp.float32),
+        ),
+        in_specs=[vmem] * 6,
+        out_specs=[vmem] * 3,
+        scratch_shapes=[
+            blocks(half), blocks(half), blocks(half), blocks(sections), blocks(lines),
+            blocks(lines), blocks(lines),
+            pltpu.VMEM((steps + 1, experts, 8, rows), jnp.float32),
+            pltpu.VMEM((steps, experts, 8, rows), jnp.float32),
+            dma((2, half)), dma((2, half)), dma((2, sections)), dma((2, sections)),
+            dma((2, lines)), dma((2, lines)), dma((2, lines)), dma((2, lines)),
+            dma((2, lines)), dma((2, lines)), dma((steps,)), dma((steps,)),
+        ],
+        compiler_params=pltpu.CompilerParams(
+            collective_id=1, has_side_effects=True, vmem_limit_bytes=VMEM_BYTES
+        ),
+        name="return_rows",
+    )(part_y, part_z, select, inner, tokens, upstream)
+
+
+def slot_targets(route_rows, capacity, experts):
+    tok_count, top_count = route_rows.shape
+    flat_routes = route_rows.reshape(-1)
+    onehot = (flat_routes[:, None] == jnp.arange(experts, dtype=jnp.int32)[None, :]).astype(
+        jnp.int32
+    )
+    earlier = jnp.cumsum(onehot, axis=0) - onehot
+    position = jnp.sum(earlier * onehot, axis=1)
+    return (flat_routes * capacity + position).reshape(tok_count, top_count)
+
+
+def across(a, b):
+    return lax.dot_general(a, b, (((1,), (1,)), ((), ())), preferred_element_type=jnp.float32)
+
+
+def down(a, b):
+    return lax.dot_general(
+        a, b, (((0,), (0,)), ((), ())), preferred_element_type=jnp.float32
+    ).astype(jnp.bfloat16)
+
+
+def by_tokens(tokens, routes, mix_weights, w_gate, w_up, w_down, upstream):
+    experts, sections = lax.axis_size("expert"), lax.axis_size("section")
+    tok_count, top_count = routes.shape
+    capacity = 5 * tok_count * top_count // (4 * experts)
+    target = slot_targets(routes, capacity, experts)
+    meta = jnp.concatenate(
+        [target.T.astype(jnp.float32), mix_weights.T, jnp.zeros((4, tok_count), jnp.float32)]
+    )
+    rows_in, rows_up, select, scale = gather_rows(
+        meta, tokens, upstream, sections, experts, capacity
+    )
+    gate_local, up_local, down_local = w_gate[0], w_up[0], w_down[0]
+    act_gate = jnp.dot(rows_in, gate_local, preferred_element_type=jnp.float32)
+    act_up = jnp.dot(rows_in, up_local, preferred_element_type=jnp.float32)
+    raw = across(rows_up, down_local)
+    sig = jax.nn.sigmoid(act_gate)
+    silu_gate = act_gate * sig
+    hidden = silu_gate * act_up
+    inner = jnp.sum(hidden * raw, axis=1, keepdims=True)
+    hidden = (hidden * scale).astype(jnp.bfloat16)
+    grad_hidden = raw * scale
+    dsilu = sig * (1.0 + act_gate * (1.0 - sig))
+    grad_act_gate = (grad_hidden * act_up * dsilu).astype(jnp.bfloat16)
+    grad_act_up = (grad_hidden * silu_gate).astype(jnp.bfloat16)
+    part_y = jnp.dot(hidden, down_local, preferred_element_type=jnp.float32).astype(jnp.bfloat16)
+    part_z = (across(grad_act_gate, gate_local) + across(grad_act_up, up_local)).astype(
+        jnp.bfloat16
+    )
+    grad_down = down(hidden, rows_up)
+    grad_gate = down(rows_in, grad_act_gate)
+    grad_up = down(rows_in, grad_act_up)
+    mixed, grad_tokens, table = return_rows(
+        part_y, part_z, select, inner, tokens, upstream, sections, experts, capacity
+    )
+    chosen = routes[:, :, None] == jnp.arange(experts, dtype=jnp.int32)
+    grad_mix = jnp.sum(jnp.where(chosen, table[:experts].T[:, None, :], 0.0), axis=2)
+    return (mixed, grad_tokens, grad_mix, grad_gate[None], grad_up[None], grad_down[None])
 
 
 def slot_tables(route_rows, mix_rows, capacity, experts):
@@ -25,7 +534,7 @@
     return (target, select, weighted, slot_token)
 
 
-def per_device(tokens, routes, mix_weights, w_gate, w_up, w_down, upstream):
+def by_slots(tokens, routes, mix_weights, w_gate, w_up, w_down, upstream):
     experts = lax.axis_size("expert")
     tok_count = tokens.shape[0]
     top_count = routes.shape[1]
@@ -100,6 +609,15 @@
     grad_moe = jnp.dot(select.T, back_rows, precision=highest)
     grad_tokens = (upstream_wide + grad_moe).astype(jnp.bfloat16)
     return (mixed, grad_tokens, grad_mix, grad_gate[None], grad_up[None], grad_down[None])
+
+
+def per_device(*arrays):
+    tokens, routes = arrays[:2]
+    experts = lax.axis_size("expert")
+    slots = 5 * tokens.shape[0] * routes.shape[1] // 4
+    if experts * tokens.shape[0] <= 2 * slots:
+        return by_tokens(*arrays)
+    return by_slots(*arrays)
 
 
 def solution(mesh):

time: 483 us -> 329 us (0.68)
  waiting for transfers between devices: 292 us -> 0 us
  Pallas kernels: 0 us -> 224 us
  blocking collectives: 48.5 us -> 0 us
  between operations: 14 us -> 0.76 us
  local copies, waits for them, and re-layouts: 13.4 us -> 4.64 us
  matrix products: 103 us -> 94.6 us
  starting transfers between devices: 7.53 us -> 0 us
    pallas_call x0 -> x2, Pallas kernels: none -> 224 us  [the longest x1 130 us: return_rows(): pl.pallas_call(functools.partial(return_kernel, sections, experts, cap),...]
    all_gather x2 -> x0, waiting for transfers between devices: 148 us -> none  [to_experts(): whole = lax.all_gather(arrived, 'section', axis=2, tiled=True)]
    reduce_scatter x2 -> x0, waiting for transfers between devices: 144 us -> none  [to_sources(): lax.psum_scatter(partial_value.reshape(experts, capacity, -1).astype(jnp....]
    all_to_all x2 -> x0, blocking collectives: 27.7 us -> none  [to_experts(): lax.all_to_all(block.reshape(experts, capacity, -1), 'expert', split_axis...]
    psum x1 -> x0, blocking collectives: 20.7 us -> none  [per_device(): grad_mix = lax.psum(mix_terms, 'section')]
    gather x4 -> x0, local copies, waits for them, and re-layouts: 10.2 us -> none  [the longest x2 5.58 us: collect(): taken = source[slot_token].astype(jnp.float32)]
    dot_general x12 -> x9, matrix products: 103 us -> 94.6 us  [the longest x3 37.8 us: across(): lax.dot_general(a, b, (((1,), (1,)), ((), ())), preferred_element_type=jn...]
    all_to_all x2 -> x0, starting transfers between devices: 6.96 us -> none  [to_sources(): lax.all_to_all(summed, 'expert', split_axis=0, concat_axis=0, tiled=True)]
  transfers between devices with their start and end apart: 6 -> 0, of which waited for: 4 -> 0; matrix products, arithmetic and copies ran while one was open for 17% -> 0% of each run, Pallas kernels for 0% -> 0%
where the time goes in v1:
time: 329 us; the launch traced here: 328 us
  Pallas kernels  224 us (68%)
  matrix products  94.6 us (29%)
  local copies, waits for them, and re-layouts  4.64 us (1%)
  other arithmetic  4.32 us (1%)
    pallas_call x1, Pallas kernels, return_rows(): pl.pallas_call(functools.partial(return_kernel, sections, experts, cap),...  130 us
    pallas_call x1, Pallas kernels, gather_rows(): pl.pallas_call(functools.partial(gather_kernel, sections, experts, cap),...  93.9 us
    dot_general x3, matrix products, across(): lax.dot_general(a, b, (((1,), (1,)), ((), ())), preferred_element_type=jn...  37.8 us
    dot_general x3, matrix products, down(): lax.dot_general(a, b, (((0,), (0,)), ((), ())), preferred_element_type=jn...  29.8 us
    dot_general x1, matrix products, by_tokens(): act_gate = jnp.dot(rows_in, gate_local, preferred_element_type=jnp.float32)  10.7 us
    dot_general x1, matrix products, by_tokens(): act_up = jnp.dot(rows_in, up_local, preferred_element_type=jnp.float32)  9.03 us
    dot_general x1, matrix products, by_tokens(): jnp.dot(hidden, down_local, preferred_element_type=jnp.float32)  7.28 us

profile of v1, /device:TPU:0, one launch (start us, length us, event | category | flops | bytes accessed | tf_op | source)
XLA Modules:
  0.0 328.3 jit_solution(17619544687969463431)
XLA Ops:
  0.6 0.8 copy.21
  1.4 0.1 eq.42
  1.6 1.2 reduce-window.6
  2.8 0.2 slice_reduce_fusion
  3.0 0.2 reduce-window.9
  3.2 0.1 add_bitcast_fusion
  3.3 0.1 eq.38
  3.5 0.1 reduce_sum.30
  3.6 0.1 copy.23
  3.7 0.7 convert_bitcast_fusion.3
  4.4 0.1 pad.2.clone
  4.5 1.3 maximum_maximum_fusion.meta_ref
  5.8 93.9 %gather_rows.1 = (bf16[640,4096]{1,0:T(8,128)(2,1)}, bf16[640,4096]{1,0:T(8,128)(2,1)}, bf16[640,256]{1,0:T(8,128)(2,1)}, f32[640,1]{1,0:T(8,128)}) custom-call(f32[8,256]{1,0:T(8,128)} %maximum_maximum_fusion.meta_ref, bf16[256,512]{1,0:T(8,128)(2,1)} %tok_ref.3, bf16[256,512]{1,0:T(8,128)(2,1)} %up_ref.3), custom_call_target="tpu_custom_call" | custom-call | tf_op jit(solution)/shard_map/gather_rows/pallas_call | solution.py:185
  99.7 0.0 copy-start.4
  99.8 10.7 %fusion.10 = f32[640,1024]{1,0:T(8,128)} fusion(bf16[640,4096]{1,0:T(8,128)(2,1)} %get-tuple-element.13, bf16[1,4096,1024]{2,1,0:T(8,128)(2,1)} %param.10), kind=kOutput, calls=%fused_computation.11 | convolution fusion | flops 5368709120 | bytes 16252928 | tf_op jit(solution)/shard_map/dot_general | solution.py:491
  110.5 0.0 copy-done.4
  110.5 0.0 copy-start
  110.5 9.0 %fusion.6 = f32[640,1024]{1,0:T(8,128)} fusion(bf16[640,4096]{1,0:T(8,128)(2,1)S(1)} %copy-done.4, bf16[1,4096,1024]{2,1,0:T(8,128)(2,1)} %param.11), kind=kOutput, calls=%fused_computation.7 | convolution fusion | flops 5368709120 | bytes 16252928 | tf_op jit(solution)/shard_map/dot_general | solution.py:492
  119.5 0.0 copy-done
  119.5 0.2 reduce.1
  119.7 12.8 %multiply_reduce_fusion = (f32[640]{0:T(1024)S(1)}, bf16[640,1024]{1,0:T(8,128)(2,1)}, bf16[640,1024]{1,0:T(8,128)(2,1)S(1)}, bf16[640,1024]{1,0:T(8,128)(2,1)S(1)}) fusion(f32[640,1024]{1,0:T(8,128)} %fusion.6, f32[640,1024]{1,0:T(8,128)} %fusion.10, f32[640]{0:T(1024)S(1)} %reduce.1, bf16[640,4096]{1,0:T(8,128)(2,1)} %get-tuple-element.15, ...), kind=kOutput, calls=%fused_computation.17 | convolution fusion | flops 5381160448 | bytes 22811648 | tf_op jit(solution)/shard_map/dot_general | solution.py:470
  132.5 0.0 copy-start.5
  132.5 0.0 slice-start
  132.5 12.2 %fusion.4 = f32[640,4096]{1,0:T(8,128)} fusion(bf16[640,1024]{1,0:T(8,128)(2,1)S(1)} %get-tuple-element.23, bf16[1,4096,1024]{2,1,0:T(8,128)(2,1)} %param.11), kind=kOutput, calls=%fused_computation.5 | convolution fusion | flops 5368709120 | bytes 20185088 | tf_op jit(solution)/shard_map/dot_general | solution.py:470
  144.7 0.0 copy-done.5
  144.7 0.0 slice-start.1
  144.7 12.8 %add_convert_fusion.z_ref = bf16[640,4096]{1,0:T(8,128)(2,1)} fusion(f32[640,4096]{1,0:T(8,128)} %fusion.4, bf16[640,1024]{1,0:T(8,128)(2,1)} %get-tuple-element.21, bf16[1,4096,1024]{2,1,0:T(8,128)(2,1)} %param.10), kind=kOutput, calls=%fused_computation | convolution fusion | flops 5373952000 | bytes 25427968 | tf_op jit(solution)/shard_map/dot_general | solution.py:470
  157.5 0.0 slice-done
  157.5 0.0 slice-done.1
  157.5 7.3 %fusion.12.y_ref = bf16[640,4096]{1,0:T(8,128)(2,1)} fusion(bf16[640,1024]{1,0:T(8,128)(2,1)S(1)} %get-tuple-element.22, bf16[1,1024,4096]{2,1,0:T(8,128)(2,1)S(1)} %bitcast.66), kind=kOutput, calls=%fused_computation.16 | convolution fusion | flops 5371330560 | bytes 14942208 | tf_op jit(solution)/shard_map/dot_general | solution.py:503
  164.8 0.9 broadcast_in_dim.38.dot_ref
  165.6 0.0 copy-start.3
  165.6 0.0 copy-start.6
  165.6 0.0 slice-start.4
  165.6 130.1 %return_rows.1 = (bf16[256,512]{1,0:T(8,128)(2,1)}, bf16[256,512]{1,0:T(8,128)(2,1)}, f32[8,256]{1,0:T(8,128)}) custom-call(bf16[640,4096]{1,0:T(8,128)(2,1)} %fusion.12.y_ref, bf16[640,4096]{1,0:T(8,128)(2,1)} %add_convert_fusion.z_ref, bf16[640,256]{1,0:T(8,128)(2,1)} %get-tuple-element.16.sel_ref, f32[640,1]{1,0:T(8,128)} %broadcast_in_dim.38.dot_ref, ...), custom_call_target="tpu_custom_call" | custom-call | tf_op jit(solution)/shard_map/return_rows/pallas_call | solution.py:433
  295.7 0.7 slice_bitcast_fusion
  296.4 0.0 copy-done.3
  296.4 0.6 select_reduce_fusion
  297.0 0.0 copy-done.6
  297.0 0.0 slice-start.5
  297.0 0.0 copy-start.7
  297.0 0.0 slice-start.2
  297.0 11.7 %convert_bitcast_fusion.1 = bf16[1,4096,1024]{2,1,0:T(8,128)(2,1)} fusion(bf16[640,4096]{1,0:T(8,128)(2,1)} %get-tuple-element.13, bf16[640,1024]{1,0:T(8,128)(2,1)S(1)} %copy-done.6), kind=kOutput, calls=%fused_computation.14 | convolution fusion | flops 5372903424 | bytes 14942208 | tf_op jit(solution)/shard_map/dot_general | solution.py:474
  308.7 0.0 slice-done.4
  308.7 0.0 slice-done.5
  308.7 0.0 copy-done.7
  308.7 0.0 slice-start.3
  308.7 9.1 %convert_bitcast_fusion.2 = bf16[1,4096,1024]{2,1,0:T(8,128)(2,1)} fusion(bf16[640,4096]{1,0:T(8,128)(2,1)S(1)} %bitcast.70, bf16[640,1024]{1,0:T(8,128)(2,1)S(1)} %copy-done.7), kind=kOutput, calls=%fused_computation.15 | convolution fusion | flops 5372903424 | bytes 14942208 | tf_op jit(solution)/shard_map/dot_general | solution.py:474
  317.8 0.0 slice-done.2
  317.8 0.0 slice-done.3
  317.8 0.0 copy-start.2
  317.8 0.0 copy-start.1
  317.8 9.1 %convert_bitcast_fusion = bf16[1,1024,4096]{2,1,0:T(8,128)(2,1)} fusion(bf16[640,1024]{1,0:T(8,128)(2,1)S(1)} %get-tuple-element.22, bf16[640,4096]{1,0:T(8,128)(2,1)S(1)} %bitcast.68), kind=kOutput, calls=%fused_computation.13 | convolution fusion | flops 5372903424 | bytes 14942208 | tf_op jit(solution)/shard_map/dot_general | solution.py:474
  326.9 0.0 copy-done.2
  326.9 0.7 copy.29
  327.6 0.0 copy-done.1
  327.6 0.7 copy.30
  (6 shorter events, 0.0 us)
Async XLA Ops:
  99.7 10.7 %copy-start.4 = (bf16[640,4096]{1,0:T(8,128)(2,1)S(1)}, bf16[640,4096]{1,0:T(8,128)(2,1)}, u32[]{:S(2)}) copy-start(bf16[640,4096]{1,0:T(8,128)(2,1)} %get-tuple-element.13) | copy-start | bytes 15728644
  110.5 9.0 %copy-start = (f32[640,1]{1,0:T(8,128)S(1)}, f32[640,1]{1,0:T(8,128)}, u32[]{:S(2)}) copy-start(f32[640,1]{1,0:T(8,128)} %get-tuple-element.14) | copy-start | bytes 7684
  132.5 12.2 %copy-start.5 = (bf16[640,1024]{1,0:T(8,128)(2,1)}, bf16[640,1024]{1,0:T(8,128)(2,1)S(1)}, u32[]{:S(2)}) copy-start(bf16[640,1024]{1,0:T(8,128)(2,1)S(1)} %get-tuple-element.23) | copy-start | bytes 3932164
  132.5 25.0 %slice-start = ((s8[8388608]{0:T(1024)(128)(4,1)}), s8[4194304]{0:T(1024)(128)(4,1)S(1)}, s32[]{:S(2)}) async-start(s8[8388608]{0:T(1024)(128)(4,1)} %bitcast.65), calls=%async_computation | async-start | bytes 8388608
  144.7 12.8 %slice-start.1 = ((s8[8388608]{0:T(1024)(128)(4,1)}), s8[4194304]{0:T(1024)(128)(4,1)S(1)}, s32[]{:S(2)}) async-start(s8[8388608]{0:T(1024)(128)(4,1)} %bitcast.65), calls=%async_computation.1 | async-start | bytes 8388608
  165.6 130.8 %copy-start.3 = (s32[256,2]{0,1:T(2,128)S(1)}, s32[256,2]{0,1:T(2,128)}, u32[]{:S(2)}) copy-start(s32[256,2]{0,1:T(2,128)} %param.8) | copy-start | bytes 6148
  165.6 131.4 %copy-start.6 = (bf16[640,1024]{1,0:T(8,128)(2,1)S(1)}, bf16[640,1024]{1,0:T(8,128)(2,1)}, u32[]{:S(2)}) copy-start(bf16[640,1024]{1,0:T(8,128)(2,1)} %copy-done.5) | copy-start | bytes 3932164
  165.6 143.1 %slice-start.4 = ((s8[5242880]{0:T(1024)(128)(4,1)}), s8[1048576]{0:T(1024)(128)(4,1)S(1)}, s32[]{:S(2)}) async-start(s8[5242880]{0:T(1024)(128)(4,1)} %bitcast.69), calls=%async_computation.4 | async-start | bytes 2097152
  297.0 11.7 %slice-start.5 = ((s8[5242880]{0:T(1024)(128)(4,1)}), s8[4194304]{0:T(1024)(128)(4,1)S(1)}, s32[]{:S(2)}) async-start(s8[5242880]{0:T(1024)(128)(4,1)} %bitcast.69), calls=%async_computation.5 | async-start | bytes 8388608
  297.0 11.7 %copy-start.7 = (bf16[640,1024]{1,0:T(8,128)(2,1)S(1)}, bf16[640,1024]{1,0:T(8,128)(2,1)}, u32[]{:S(2)}) copy-start(bf16[640,1024]{1,0:T(8,128)(2,1)} %get-tuple-element.21) | copy-start | bytes 3932164
  297.0 20.8 %slice-start.2 = ((s8[5242880]{0:T(1024)(128)(4,1)}), s8[4194304]{0:T(1024)(128)(4,1)S(1)}, s32[]{:S(2)}) async-start(s8[5242880]{0:T(1024)(128)(4,1)} %bitcast.67), calls=%async_computation.2 | async-start | bytes 8388608
  308.7 9.1 %slice-start.3 = ((s8[5242880]{0:T(1024)(128)(4,1)}), s8[1048576]{0:T(1024)(128)(4,1)S(1)}, s32[]{:S(2)}) async-start(s8[5242880]{0:T(1024)(128)(4,1)} %bitcast.67), calls=%async_computation.3 | async-start | bytes 2097152
  317.8 9.1 %copy-start.2 = (bf16[256,512]{1,0:T(8,128)(2,1)S(1)}, bf16[256,512]{1,0:T(8,128)(2,1)}, u32[]{:S(2)}) copy-start(bf16[256,512]{1,0:T(8,128)(2,1)} %get-tuple-element.30) | copy-start | bytes 786436
  317.8 9.8 %copy-start.1 = (bf16[256,512]{1,0:T(8,128)(2,1)S(1)}, bf16[256,512]{1,0:T(8,128)(2,1)}, u32[]{:S(2)}) copy-start(bf16[256,512]{1,0:T(8,128)(2,1)} %get-tuple-element.31) | copy-start | bytes 786436

commit v2 on v1

--- a/solution.py
+++ b/solution.py
@@ -156,21 +156,26 @@
             first * table[2:3, :] + second * table[3:4, :], axis=1, keepdims=True
         )
 
+    def dispatch(s, which):
+        columns = pl.ds(pl.multiple_of(s * width, width), width)
+        for half in range(experts // 2):
+            b = 2 * half + which
+            at = pl.ds(pl.multiple_of(b * cap, 16), cap)
+            for a, out in enumerate((x_ref, u_ref)):
+                out[at, columns] = jnp.dot(
+                    sel_ref[at, :], held[a][b * sections + s], preferred_element_type=jnp.float32
+                ).astype(jnp.bfloat16)
+
+    @pl.loop(0, sections)
+    def _(s):
+        dispatch(s, core)
+
     @pl.loop(0, sections)
     def _(s):
         for a in range(2):
             for half in range(experts // 2):
                 arrive(a, (2 * half + 1 - core) * sections + s)
-
-    @pl.loop(0, sections)
-    def _(s):
-        columns = pl.ds(pl.multiple_of(s * width, width), width)
-        for b in range(experts):
-            take = sel_ref[b * cap : (b + 1) * cap, :]
-            for source, out in ((tok_all, x_ref), (up_all, u_ref)):
-                out[b * cap : (b + 1) * cap, columns] = jnp.dot(
-                    take, source[b * sections + s], preferred_element_type=jnp.float32
-                ).astype(jnp.bfloat16)
+        dispatch(s, 1 - core)
 
     walk(lambda c: c.wait_send(), lambda a, block: None)
     for j in range(experts - 1):
@@ -299,16 +304,21 @@
         tab_out[0, b] = jnp.where(line == here.expert, sums, 0.0)
     table_copy(0).start()
 
+    def ends_first(i):
+        return lax.div(i, 2) + lax.rem(i, 2) * (lines - 1 - 2 * lax.div(i, 2))
+
     def offer(fx, fy):
         @pl.loop(0, lines)
-        def _(zz):
+        def _(i):
+            zz = ends_first(i)
             for a in range(2):
                 out[a, number(fx, fy, zz)] = to_tokens(a, fx, fy, zz, 1 - core).astype(jnp.bfloat16)
                 to_mate(a, fx, fy, zz).start()
 
     def join(fx, fy):
         @pl.loop(0, lines)
-        def _(zz):
+        def _(i):
+            zz = ends_first(i)
             for a in range(2):
                 q = number(fx, fy, zz)
                 mine = to_tokens(a, fx, fy, zz, core)
@@ -318,17 +328,22 @@
                     to_first(a, fx, fy, zz).start()
 
     offer(1, 1)
+    table_step(0)
     offer(0, 1)
+    table_step(1)
     join(1, 1)
+    table_step(2)
     offer(1, 0)
     join(0, 1)
     offer(0, 0)
     join(1, 0)
     join(0, 0)
-    table_step(0)
+    for i in range(3, len(partners)):
+        table_step(i)
 
     @pl.loop(0, lines)
-    def _(zz):
+    def _(i):
+        zz = ends_first(i)
         for a in range(2):
             fx, fy = (1, 0) if a == 0 else (0, 1)
             to_first(a, fx, fy, zz).wait_recv()
@@ -336,8 +351,6 @@
             add(a, number(fx, fy, zz), got1[a, slot])
             to_second(a, fx, fy, zz).start()
 
-    table_step(1)
-
     @pl.loop(0, lines)
     def _(zz):
         for a in range(2):
@@ -345,8 +358,6 @@
             slot = (x if a == 0 else y) * lines + zz
             add(a, number(0, 0, zz), got1[a, slot])
 
-    table_step(2)
-
     def both(do):
         for up, down in zip(range(lines - 1, 0, -1), range(lines - 1)):
 
@@ -382,8 +393,6 @@
             to_down(a, zz).start()
 
     both(pass_on)
-    for i in range(3, len(partners)):
-        table_step(i)
     gmix_ref[...] = tab_out[len(partners), here.expert]
 
     for a, (base, result) in enumerate(((tok_ref, mixed_ref), (up_ref, gtok_ref))):

time: 329 us -> 312 us (0.948)
  Pallas kernels: 224 us -> 206 us
    pallas_call x1, Pallas kernels: 130 us -> 110 us  [return_rows(): pl.pallas_call(functools.partial(return_kernel, sections, experts, cap),...]
where the time goes in v2:
time: 312 us; the launch traced here: 310 us
  Pallas kernels  206 us (66%)
  matrix products  94.6 us (30%)
  local copies, waits for them, and re-layouts  4.64 us (1%)
  other arithmetic  4.32 us (1%)
    pallas_call x1, Pallas kernels, return_rows(): pl.pallas_call(functools.partial(return_kernel, sections, experts, cap),...  110 us
    pallas_call x1, Pallas kernels, gather_rows(): pl.pallas_call(functools.partial(gather_kernel, sections, experts, cap),...  95.2 us
    dot_general x3, matrix products, across(): lax.dot_general(a, b, (((1,), (1,)), ((), ())), preferred_element_type=jn...  37.8 us
    dot_general x3, matrix products, down(): lax.dot_general(a, b, (((0,), (0,)), ((), ())), preferred_element_type=jn...  29.8 us
    dot_general x1, matrix products, by_tokens(): act_gate = jnp.dot(rows_in, gate_local, preferred_element_type=jnp.float32)  10.7 us
    dot_general x1, matrix products, by_tokens(): act_up = jnp.dot(rows_in, up_local, preferred_element_type=jnp.float32)  9.03 us
    dot_general x1, matrix products, by_tokens(): jnp.dot(hidden, down_local, preferred_element_type=jnp.float32)  7.28 us

profile of v2, /device:TPU:0, one launch (start us, length us, event | category | flops | bytes accessed | tf_op | source)
XLA Modules:
  0.0 310.0 jit_solution(5196344686886449455)
XLA Ops:
  0.6 0.8 copy.21
  1.4 0.1 eq.42
  1.6 1.2 reduce-window.6
  2.8 0.2 slice_reduce_fusion
  3.0 0.2 reduce-window.9
  3.2 0.1 add_bitcast_fusion
  3.3 0.1 eq.38
  3.5 0.1 reduce_sum.30
  3.6 0.1 copy.23
  3.7 0.7 convert_bitcast_fusion.3
  4.4 0.1 pad.2.clone
  4.5 1.3 maximum_maximum_fusion.meta_ref
  5.8 95.2 %gather_rows.1 = (bf16[640,4096]{1,0:T(8,128)(2,1)}, bf16[640,4096]{1,0:T(8,128)(2,1)}, bf16[640,256]{1,0:T(8,128)(2,1)}, f32[640,1]{1,0:T(8,128)}) custom-call(f32[8,256]{1,0:T(8,128)} %maximum_maximum_fusion.meta_ref, bf16[256,512]{1,0:T(8,128)(2,1)} %tok_ref.3, bf16[256,512]{1,0:T(8,128)(2,1)} %up_ref.3), custom_call_target="tpu_custom_call" | custom-call | tf_op jit(solution)/shard_map/gather_rows/pallas_call | solution.py:190
  101.1 0.0 copy-start.4
  101.1 10.7 %fusion.10 = f32[640,1024]{1,0:T(8,128)} fusion(bf16[640,4096]{1,0:T(8,128)(2,1)} %get-tuple-element.13, bf16[1,4096,1024]{2,1,0:T(8,128)(2,1)} %param.10), kind=kOutput, calls=%fused_computation.11 | convolution fusion | flops 5368709120 | bytes 16252928 | tf_op jit(solution)/shard_map/dot_general | solution.py:500
  111.8 0.0 copy-done.4
  111.8 0.0 copy-start
  111.8 9.0 %fusion.6 = f32[640,1024]{1,0:T(8,128)} fusion(bf16[640,4096]{1,0:T(8,128)(2,1)S(1)} %copy-done.4, bf16[1,4096,1024]{2,1,0:T(8,128)(2,1)} %param.11), kind=kOutput, calls=%fused_computation.7 | convolution fusion | flops 5368709120 | bytes 16252928 | tf_op jit(solution)/shard_map/dot_general | solution.py:501
  120.8 0.0 copy-done
  120.8 0.2 reduce.1
  121.0 12.8 %multiply_reduce_fusion = (f32[640]{0:T(1024)S(1)}, bf16[640,1024]{1,0:T(8,128)(2,1)}, bf16[640,1024]{1,0:T(8,128)(2,1)S(1)}, bf16[640,1024]{1,0:T(8,128)(2,1)S(1)}) fusion(f32[640,1024]{1,0:T(8,128)} %fusion.6, f32[640,1024]{1,0:T(8,128)} %fusion.10, f32[640]{0:T(1024)S(1)} %reduce.1, bf16[640,4096]{1,0:T(8,128)(2,1)} %get-tuple-element.15, ...), kind=kOutput, calls=%fused_computation.17 | convolution fusion | flops 5381160448 | bytes 22811648 | tf_op jit(solution)/shard_map/dot_general | solution.py:479
  133.8 0.0 copy-start.5
  133.8 0.0 slice-start
  133.8 12.2 %fusion.4 = f32[640,4096]{1,0:T(8,128)} fusion(bf16[640,1024]{1,0:T(8,128)(2,1)S(1)} %get-tuple-element.23, bf16[1,4096,1024]{2,1,0:T(8,128)(2,1)} %param.11), kind=kOutput, calls=%fused_computation.5 | convolution fusion | flops 5368709120 | bytes 20185088 | tf_op jit(solution)/shard_map/dot_general | solution.py:479
  146.0 0.0 copy-done.5
  146.0 0.0 slice-start.1
  146.0 12.8 %add_convert_fusion.z_ref = bf16[640,4096]{1,0:T(8,128)(2,1)} fusion(f32[640,4096]{1,0:T(8,128)} %fusion.4, bf16[640,1024]{1,0:T(8,128)(2,1)} %get-tuple-element.21, bf16[1,4096,1024]{2,1,0:T(8,128)(2,1)} %param.10), kind=kOutput, calls=%fused_computation | convolution fusion | flops 5373952000 | bytes 25427968 | tf_op jit(solution)/shard_map/dot_general | solution.py:479
  158.8 0.0 slice-done
  158.8 0.0 slice-done.1
  158.8 7.3 %fusion.12.y_ref = bf16[640,4096]{1,0:T(8,128)(2,1)} fusion(bf16[640,1024]{1,0:T(8,128)(2,1)S(1)} %get-tuple-element.22, bf16[1,1024,4096]{2,1,0:T(8,128)(2,1)S(1)} %bitcast.66), kind=kOutput, calls=%fused_computation.16 | convolution fusion | flops 5371330560 | bytes 14942208 | tf_op jit(solution)/shard_map/dot_general | solution.py:512
  166.1 0.9 broadcast_in_dim.38.dot_ref
  166.9 0.0 copy-start.3
  167.0 0.0 copy-start.6
  167.0 0.0 slice-start.4
  167.0 110.4 %return_rows.1 = (bf16[256,512]{1,0:T(8,128)(2,1)}, bf16[256,512]{1,0:T(8,128)(2,1)}, f32[8,256]{1,0:T(8,128)}) custom-call(bf16[640,4096]{1,0:T(8,128)(2,1)} %fusion.12.y_ref, bf16[640,4096]{1,0:T(8,128)(2,1)} %add_convert_fusion.z_ref, bf16[640,256]{1,0:T(8,128)(2,1)} %get-tuple-element.16.sel_ref, f32[640,1]{1,0:T(8,128)} %broadcast_in_dim.38.dot_ref, ...), custom_call_target="tpu_custom_call" | custom-call | tf_op jit(solution)/shard_map/return_rows/pallas_call | solution.py:442
  277.4 0.7 slice_bitcast_fusion
  278.1 0.0 copy-done.3
  278.1 0.6 select_reduce_fusion
  278.7 0.0 copy-done.6
  278.7 0.0 slice-start.5
  278.7 0.0 copy-start.7
  278.7 0.0 slice-start.2
  278.7 11.7 %convert_bitcast_fusion.1 = bf16[1,4096,1024]{2,1,0:T(8,128)(2,1)} fusion(bf16[640,4096]{1,0:T(8,128)(2,1)} %get-tuple-element.13, bf16[640,1024]{1,0:T(8,128)(2,1)S(1)} %copy-done.6), kind=kOutput, calls=%fused_computation.14 | convolution fusion | flops 5372903424 | bytes 14942208 | tf_op jit(solution)/shard_map/dot_general | solution.py:483
  290.4 0.0 slice-done.4
  290.4 0.0 slice-done.5
  290.4 0.0 copy-done.7
  290.4 0.0 slice-start.3
  290.4 9.1 %convert_bitcast_fusion.2 = bf16[1,4096,1024]{2,1,0:T(8,128)(2,1)} fusion(bf16[640,4096]{1,0:T(8,128)(2,1)S(1)} %bitcast.70, bf16[640,1024]{1,0:T(8,128)(2,1)S(1)} %copy-done.7), kind=kOutput, calls=%fused_computation.15 | convolution fusion | flops 5372903424 | bytes 14942208 | tf_op jit(solution)/shard_map/dot_general | solution.py:483
  299.5 0.0 slice-done.2
  299.5 0.0 slice-done.3
  299.5 0.0 copy-start.2
  299.5 0.0 copy-start.1
  299.5 9.1 %convert_bitcast_fusion = bf16[1,1024,4096]{2,1,0:T(8,128)(2,1)} fusion(bf16[640,1024]{1,0:T(8,128)(2,1)S(1)} %get-tuple-element.22, bf16[640,4096]{1,0:T(8,128)(2,1)S(1)} %bitcast.68), kind=kOutput, calls=%fused_computation.13 | convolution fusion | flops 5372903424 | bytes 14942208 | tf_op jit(solution)/shard_map/dot_general | solution.py:483
  308.6 0.0 copy-done.2
  308.6 0.7 copy.29
  309.3 0.0 copy-done.1
  309.3 0.7 copy.30
  (6 shorter events, 0.0 us)
Async XLA Ops:
  101.1 10.7 %copy-start.4 = (bf16[640,4096]{1,0:T(8,128)(2,1)S(1)}, bf16[640,4096]{1,0:T(8,128)(2,1)}, u32[]{:S(2)}) copy-start(bf16[640,4096]{1,0:T(8,128)(2,1)} %get-tuple-element.13) | copy-start | bytes 15728644
  111.8 9.0 %copy-start = (f32[640,1]{1,0:T(8,128)S(1)}, f32[640,1]{1,0:T(8,128)}, u32[]{:S(2)}) copy-start(f32[640,1]{1,0:T(8,128)} %get-tuple-element.14) | copy-start | bytes 7684
  133.8 12.2 %copy-start.5 = (bf16[640,1024]{1,0:T(8,128)(2,1)}, bf16[640,1024]{1,0:T(8,128)(2,1)S(1)}, u32[]{:S(2)}) copy-start(bf16[640,1024]{1,0:T(8,128)(2,1)S(1)} %get-tuple-element.23) | copy-start | bytes 3932164
  133.8 25.0 %slice-start = ((s8[8388608]{0:T(1024)(128)(4,1)}), s8[4194304]{0:T(1024)(128)(4,1)S(1)}, s32[]{:S(2)}) async-start(s8[8388608]{0:T(1024)(128)(4,1)} %bitcast.65), calls=%async_computation | async-start | bytes 8388608
  146.0 12.8 %slice-start.1 = ((s8[8388608]{0:T(1024)(128)(4,1)}), s8[4194304]{0:T(1024)(128)(4,1)S(1)}, s32[]{:S(2)}) async-start(s8[8388608]{0:T(1024)(128)(4,1)} %bitcast.65), calls=%async_computation.1 | async-start | bytes 8388608
  166.9 111.1 %copy-start.3 = (s32[256,2]{0,1:T(2,128)S(1)}, s32[256,2]{0,1:T(2,128)}, u32[]{:S(2)}) copy-start(s32[256,2]{0,1:T(2,128)} %param.8) | copy-start | bytes 6148
  167.0 111.7 %copy-start.6 = (bf16[640,1024]{1,0:T(8,128)(2,1)S(1)}, bf16[640,1024]{1,0:T(8,128)(2,1)}, u32[]{:S(2)}) copy-start(bf16[640,1024]{1,0:T(8,128)(2,1)} %copy-done.5) | copy-start | bytes 3932164
  167.0 123.4 %slice-start.4 = ((s8[5242880]{0:T(1024)(128)(4,1)}), s8[1048576]{0:T(1024)(128)(4,1)S(1)}, s32[]{:S(2)}) async-start(s8[5242880]{0:T(1024)(128)(4,1)} %bitcast.69), calls=%async_computation.4 | async-start | bytes 2097152
  278.7 11.7 %slice-start.5 = ((s8[5242880]{0:T(1024)(128)(4,1)}), s8[4194304]{0:T(1024)(128)(4,1)S(1)}, s32[]{:S(2)}) async-start(s8[5242880]{0:T(1024)(128)(4,1)} %bitcast.69), calls=%async_computation.5 | async-start | bytes 8388608
  278.7 11.7 %copy-start.7 = (bf16[640,1024]{1,0:T(8,128)(2,1)S(1)}, bf16[640,1024]{1,0:T(8,128)(2,1)}, u32[]{:S(2)}) copy-start(bf16[640,1024]{1,0:T(8,128)(2,1)} %get-tuple-element.21) | copy-start | bytes 3932164
  278.7 20.8 %slice-start.2 = ((s8[5242880]{0:T(1024)(128)(4,1)}), s8[4194304]{0:T(1024)(128)(4,1)S(1)}, s32[]{:S(2)}) async-start(s8[5242880]{0:T(1024)(128)(4,1)} %bitcast.67), calls=%async_computation.2 | async-start | bytes 8388608
  290.4 9.1 %slice-start.3 = ((s8[5242880]{0:T(1024)(128)(4,1)}), s8[1048576]{0:T(1024)(128)(4,1)S(1)}, s32[]{:S(2)}) async-start(s8[5242880]{0:T(1024)(128)(4,1)} %bitcast.67), calls=%async_computation.3 | async-start | bytes 2097152
  299.5 9.1 %copy-start.2 = (bf16[256,512]{1,0:T(8,128)(2,1)S(1)}, bf16[256,512]{1,0:T(8,128)(2,1)}, u32[]{:S(2)}) copy-start(bf16[256,512]{1,0:T(8,128)(2,1)} %get-tuple-element.30) | copy-start | bytes 786436
  299.5 9.8 %copy-start.1 = (bf16[256,512]{1,0:T(8,128)(2,1)S(1)}, bf16[256,512]{1,0:T(8,128)(2,1)}, u32[]{:S(2)}) copy-start(bf16[256,512]{1,0:T(8,128)(2,1)} %get-tuple-element.31) | copy-start | bytes 786436

commit v3 on v2

--- a/solution.py
+++ b/solution.py
@@ -214,7 +214,7 @@
 
 
 def return_kernel(
-    sections, experts, cap, y_ref, z_ref, sel_ref, dot_ref, tok_ref, up_ref,
+    sections, experts, cap, y_ref, z_ref, sel_ref, turn_ref, dot_ref, tok_ref, up_ref,
     mixed_ref, gtok_ref, gmix_ref,
     out, mate, acc, got1, got2, got_up, got_down, tab_out, tab_in,
     mate_s, mate_r, one_s, one_r, two_s, two_r, up_s, up_r, down_s, down_r, tab_s, tab_r,
@@ -250,9 +250,8 @@
         b = 2 * flip(y, fy) + which
         at = pl.ds(pl.multiple_of(b * cap, 16), cap)
         columns = pl.ds(pl.multiple_of((2 * zz + flip(x, fx)) * width, width), width)
-        return lax.dot_general(
-            sel_ref[at, :], parts[a][at, columns], (((0,), (0,)), ((), ())),
-            preferred_element_type=jnp.float32,
+        return jnp.dot(
+            turn_ref[b], parts[a][at, columns], preferred_element_type=jnp.float32
         )
 
     def to_mate(a, fx, fy, zz):
@@ -432,6 +431,7 @@
 def return_rows(part_y, part_z, select, inner, tokens, upstream, sections, experts, cap):
     rows, width = tokens.shape
     lines, half = sections // 2, sections * experts // 2
+    turned = select.reshape(experts, cap, rows).transpose(0, 2, 1)
     steps = 3 + (lines - 1).bit_length()
     vmem = pl.BlockSpec(memory_space=pltpu.VMEM)
     dma = pltpu.SemaphoreType.DMA
@@ -446,7 +446,7 @@
             jax.ShapeDtypeStruct(tokens.shape, jnp.bfloat16),
             jax.ShapeDtypeStruct((8, rows), jnp.float32),
         ),
-        in_specs=[vmem] * 6,
+        in_specs=[vmem] * 7,
         out_specs=[vmem] * 3,
         scratch_shapes=[
             blocks(half), blocks(half), blocks(half), blocks(sections), blocks(lines),
@@ -461,7 +461,7 @@
             collective_id=1, has_side_effects=True, vmem_limit_bytes=VMEM_BYTES
         ),
         name="return_rows",
-    )(part_y, part_z, select, inner, tokens, upstream)
+    )(part_y, part_z, select, turned, inner, tokens, upstream)
 
 
 def slot_targets(route_rows, capacity, experts):

time: 312 us -> 314 us (level)
    dot_general x1, matrix products: 7.28 us -> 10.7 us  [by_tokens(): jnp.dot(hidden, down_local, preferred_element_type=jnp.float32)]
where the time goes in v3:
time: 314 us; the launch traced here: 313 us
  Pallas kernels  205 us (65%)
  matrix products  96.8 us (31%)
  local copies, waits for them, and re-layouts  5.63 us (2%)
  other arithmetic  4.32 us (1%)
    pallas_call x1, Pallas kernels, return_rows(): pl.pallas_call(functools.partial(return_kernel, sections, experts, cap),...  110 us
    pallas_call x1, Pallas kernels, gather_rows(): pl.pallas_call(functools.partial(gather_kernel, sections, experts, cap),...  95.2 us
    dot_general x3, matrix products, across(): lax.dot_general(a, b, (((1,), (1,)), ((), ())), preferred_element_type=jn...  36.5 us
    dot_general x3, matrix products, down(): lax.dot_general(a, b, (((0,), (0,)), ((), ())), preferred_element_type=jn...  29.8 us
    dot_general x1, matrix products, by_tokens(): jnp.dot(hidden, down_local, preferred_element_type=jnp.float32)  10.7 us
    dot_general x1, matrix products, by_tokens(): act_gate = jnp.dot(rows_in, gate_local, preferred_element_type=jnp.float32)  10.7 us
    dot_general x1, matrix products, by_tokens(): act_up = jnp.dot(rows_in, up_local, preferred_element_type=jnp.float32)  9.03 us

profile of v3, /device:TPU:0, one launch (start us, length us, event | category | flops | bytes accessed | tf_op | source)
XLA Modules:
  0.0 312.9 jit_solution(1852075333331283432)
XLA Ops:
  0.6 0.8 copy.22
  1.4 0.1 eq.42
  1.6 1.2 reduce-window.6
  2.8 0.2 slice_reduce_fusion
  3.0 0.2 reduce-window.9
  3.2 0.1 add_bitcast_fusion
  3.3 0.1 eq.38
  3.5 0.1 reduce_sum.30
  3.6 0.1 copy.24
  3.7 0.7 convert_bitcast_fusion.3
  4.4 0.1 pad.2.clone
  4.5 1.3 maximum_maximum_fusion.meta_ref
  5.8 95.2 %gather_rows.1 = (bf16[640,4096]{1,0:T(8,128)(2,1)}, bf16[640,4096]{1,0:T(8,128)(2,1)}, bf16[640,256]{1,0:T(8,128)(2,1)}, f32[640,1]{1,0:T(8,128)}) custom-call(f32[8,256]{1,0:T(8,128)} %maximum_maximum_fusion.meta_ref, bf16[256,512]{1,0:T(8,128)(2,1)} %tok_ref.3, bf16[256,512]{1,0:T(8,128)(2,1)} %up_ref.3), custom_call_target="tpu_custom_call" | custom-call | tf_op jit(solution)/shard_map/gather_rows/pallas_call | solution.py:190
  101.1 0.0 copy-start.5
  101.1 10.7 %fusion.10 = f32[640,1024]{1,0:T(8,128)} fusion(bf16[640,4096]{1,0:T(8,128)(2,1)} %get-tuple-element.13, bf16[1,4096,1024]{2,1,0:T(8,128)(2,1)} %param.10), kind=kOutput, calls=%fused_computation.11 | convolution fusion | flops 5368709120 | bytes 16252928 | tf_op jit(solution)/shard_map/dot_general | solution.py:500
  111.8 0.0 copy-done.5
  111.8 0.0 copy-start.1
  111.8 9.0 %fusion.6 = f32[640,1024]{1,0:T(8,128)} fusion(bf16[640,4096]{1,0:T(8,128)(2,1)S(1)} %copy-done.5, bf16[1,4096,1024]{2,1,0:T(8,128)(2,1)} %param.11), kind=kOutput, calls=%fused_computation.7 | convolution fusion | flops 5368709120 | bytes 16252928 | tf_op jit(solution)/shard_map/dot_general | solution.py:501
  120.8 0.0 copy-done.1
  120.8 0.2 reduce.1
  121.0 12.1 %multiply_reduce_fusion = (f32[640]{0:T(1024)S(1)}, bf16[640,1024]{1,0:T(8,128)(2,1)S(1)}, bf16[640,1024]{1,0:T(8,128)(2,1)S(1)}, bf16[640,1024]{1,0:T(8,128)(2,1)S(1)}) fusion(f32[640,1024]{1,0:T(8,128)} %fusion.6, f32[640,1024]{1,0:T(8,128)} %fusion.10, f32[640]{0:T(1024)S(1)} %reduce.1, bf16[640,4096]{1,0:T(8,128)(2,1)} %get-tuple-element.15, ...), kind=kOutput, calls=%fused_computation.17 | convolution fusion | flops 5381160448 | bytes 22811648 | tf_op jit(solution)/shard_map/dot_general | solution.py:479
  133.1 0.0 copy-start.6
  133.1 12.2 %fusion.4 = f32[640,4096]{1,0:T(8,128)} fusion(bf16[640,1024]{1,0:T(8,128)(2,1)S(1)} %get-tuple-element.23, bf16[1,4096,1024]{2,1,0:T(8,128)(2,1)} %param.11), kind=kOutput, calls=%fused_computation.5 | convolution fusion | flops 5368709120 | bytes 20185088 | tf_op jit(solution)/shard_map/dot_general | solution.py:479
  145.3 0.0 copy-done.6
  145.3 12.3 %add_convert_fusion.z_ref = bf16[640,4096]{1,0:T(8,128)(2,1)} fusion(f32[640,4096]{1,0:T(8,128)} %fusion.4, bf16[640,1024]{1,0:T(8,128)(2,1)S(1)} %get-tuple-element.21, bf16[1,4096,1024]{2,1,0:T(8,128)(2,1)} %param.10), kind=kOutput, calls=%fused_computation | convolution fusion | flops 5373952000 | bytes 25427968 | tf_op jit(solution)/shard_map/dot_general | solution.py:479
  157.6 0.0 copy-start
  157.6 10.7 %fusion.12.y_ref = bf16[640,4096]{1,0:T(8,128)(2,1)} fusion(bf16[640,1024]{1,0:T(8,128)(2,1)S(1)} %get-tuple-element.22, bf16[1,1024,4096]{2,1,0:T(8,128)(2,1)} %param.12), kind=kOutput, calls=%fused_computation.16 | convolution fusion | flops 5371330560 | bytes 14942208 | tf_op jit(solution)/shard_map/dot_general | solution.py:512
  168.3 0.9 broadcast_in_dim.38.dot_ref
  169.2 0.0 copy-done
  169.2 1.0 copy.25
  170.1 0.0 copy-start.4
  170.2 0.0 slice-start.2
  170.2 110.2 %return_rows.1 = (bf16[256,512]{1,0:T(8,128)(2,1)}, bf16[256,512]{1,0:T(8,128)(2,1)}, f32[8,256]{1,0:T(8,128)}) custom-call(bf16[640,4096]{1,0:T(8,128)(2,1)} %fusion.12.y_ref, bf16[640,4096]{1,0:T(8,128)(2,1)} %add_convert_fusion.z_ref, bf16[640,256]{1,0:T(8,128)(2,1)} %get-tuple-element.16.sel_ref, bf16[4,256,160]{2,1,0:T(8,128)(2,1)} %bitcast.65, ...), custom_call_target="tpu_custom_call" | custom-call | tf_op jit(solution)/shard_map/return_rows/pallas_call | solution.py:442
  280.3 0.7 slice_bitcast_fusion
  281.0 0.0 copy-done.4
  281.0 0.6 select_reduce_fusion
  281.6 0.0 slice-start.3
  281.6 0.0 copy-start.7
  281.6 0.0 slice-start
  281.6 11.7 %convert_bitcast_fusion.1 = bf16[1,4096,1024]{2,1,0:T(8,128)(2,1)} fusion(bf16[640,4096]{1,0:T(8,128)(2,1)} %get-tuple-element.13, bf16[640,1024]{1,0:T(8,128)(2,1)S(1)} %get-tuple-element.23), kind=kOutput, calls=%fused_computation.14 | convolution fusion | flops 5372903424 | bytes 14942208 | tf_op jit(solution)/shard_map/dot_general | solution.py:483
  293.3 0.0 slice-done.2
  293.3 0.0 slice-done.3
  293.3 0.0 copy-done.7
  293.3 0.0 slice-start.1
  293.3 9.1 %convert_bitcast_fusion.2 = bf16[1,4096,1024]{2,1,0:T(8,128)(2,1)} fusion(bf16[640,4096]{1,0:T(8,128)(2,1)S(1)} %bitcast.72, bf16[640,1024]{1,0:T(8,128)(2,1)S(1)} %copy-done.7), kind=kOutput, calls=%fused_computation.15 | convolution fusion | flops 5372903424 | bytes 14942208 | tf_op jit(solution)/shard_map/dot_general | solution.py:483
  302.4 0.0 slice-done
  302.4 0.0 slice-done.1
  302.4 0.0 copy-start.3
  302.4 0.0 copy-start.2
  302.4 9.1 %convert_bitcast_fusion = bf16[1,1024,4096]{2,1,0:T(8,128)(2,1)} fusion(bf16[640,1024]{1,0:T(8,128)(2,1)S(1)} %get-tuple-element.22, bf16[640,4096]{1,0:T(8,128)(2,1)S(1)} %bitcast.70), kind=kOutput, calls=%fused_computation.13 | convolution fusion | flops 5372903424 | bytes 14942208 | tf_op jit(solution)/shard_map/dot_general | solution.py:483
  311.5 0.0 copy-done.3
  311.5 0.7 copy.31
  312.2 0.0 copy-done.2
  312.2 0.7 copy.32
  (5 shorter events, 0.0 us)
Async XLA Ops:
  101.1 10.7 %copy-start.5 = (bf16[640,4096]{1,0:T(8,128)(2,1)S(1)}, bf16[640,4096]{1,0:T(8,128)(2,1)}, u32[]{:S(2)}) copy-start(bf16[640,4096]{1,0:T(8,128)(2,1)} %get-tuple-element.13) | copy-start | bytes 15728644
  111.8 9.0 %copy-start.1 = (f32[640,1]{1,0:T(8,128)S(1)}, f32[640,1]{1,0:T(8,128)}, u32[]{:S(2)}) copy-start(f32[640,1]{1,0:T(8,128)} %get-tuple-element.14) | copy-start | bytes 7684
  133.1 12.2 %copy-start.6 = (bf16[640,1024]{1,0:T(8,128)(2,1)}, bf16[640,1024]{1,0:T(8,128)(2,1)S(1)}, u32[]{:S(2)}) copy-start(bf16[640,1024]{1,0:T(8,128)(2,1)S(1)} %get-tuple-element.21) | copy-start | bytes 3932164
  157.6 11.6 %copy-start = (bf16[640,256]{1,0:T(8,128)(2,1)S(1)}, bf16[640,256]{1,0:T(8,128)(2,1)}, u32[]{:S(2)}) copy-start(bf16[640,256]{1,0:T(8,128)(2,1)} %get-tuple-element.16.sel_ref) | copy-start | bytes 983044
  170.1 110.9 %copy-start.4 = (s32[256,2]{0,1:T(2,128)S(1)}, s32[256,2]{0,1:T(2,128)}, u32[]{:S(2)}) copy-start(s32[256,2]{0,1:T(2,128)} %param.8) | copy-start | bytes 6148
  170.2 123.2 %slice-start.2 = ((s8[5242880]{0:T(1024)(128)(4,1)}), s8[1048576]{0:T(1024)(128)(4,1)S(1)}, s32[]{:S(2)}) async-start(s8[5242880]{0:T(1024)(128)(4,1)} %bitcast.71), calls=%async_computation.2 | async-start | bytes 2097152
  281.6 11.7 %slice-start.3 = ((s8[5242880]{0:T(1024)(128)(4,1)}), s8[4194304]{0:T(1024)(128)(4,1)S(1)}, s32[]{:S(2)}) async-start(s8[5242880]{0:T(1024)(128)(4,1)} %bitcast.71), calls=%async_computation.3 | async-start | bytes 8388608
  281.6 11.7 %copy-start.7 = (bf16[640,1024]{1,0:T(8,128)(2,1)S(1)}, bf16[640,1024]{1,0:T(8,128)(2,1)}, u32[]{:S(2)}) copy-start(bf16[640,1024]{1,0:T(8,128)(2,1)} %copy-done.6) | copy-start | bytes 3932164
  281.6 20.8 %slice-start = ((s8[5242880]{0:T(1024)(128)(4,1)}), s8[4194304]{0:T(1024)(128)(4,1)S(1)}, s32[]{:S(2)}) async-start(s8[5242880]{0:T(1024)(128)(4,1)} %bitcast.69), calls=%async_computation | async-start | bytes 8388608
  293.3 9.1 %slice-start.1 = ((s8[5242880]{0:T(1024)(128)(4,1)}), s8[1048576]{0:T(1024)(128)(4,1)S(1)}, s32[]{:S(2)}) async-start(s8[5242880]{0:T(1024)(128)(4,1)} %bitcast.69), calls=%async_computation.1 | async-start | bytes 2097152
  302.4 9.1 %copy-start.3 = (bf16[256,512]{1,0:T(8,128)(2,1)S(1)}, bf16[256,512]{1,0:T(8,128)(2,1)}, u32[]{:S(2)}) copy-start(bf16[256,512]{1,0:T(8,128)(2,1)} %get-tuple-element.30) | copy-start | bytes 786436
  302.4 9.8 %copy-start.2 = (bf16[256,512]{1,0:T(8,128)(2,1)S(1)}, bf16[256,512]{1,0:T(8,128)(2,1)}, u32[]{:S(2)}) copy-start(bf16[256,512]{1,0:T(8,128)(2,1)} %get-tuple-element.31) | copy-start | bytes 786436
